TPU v7x, 256 devices: a whole 4x4x8 slice. The times are simulated.
256 devices in a mesh: seq: 64 (over x, z, core), head: 4 (over y).
Axes of the slice: x: 4, y: 4, z: 8, core: 2. Of those that a mesh axis runs over, the one named last changes fastest.
Arguments:
- image_input_rows: bfloat16 [8192, 3072], P(('seq', 'head')), may hold values from -6 to 6
- adapter_down_weight: bfloat16 [3072, 64], replicated, may hold values from -0.109375 to 0.109375
- adapter_up_weight: bfloat16 [64, 1536], replicated, may hold values from -0.75 to 0.75
- image_query_rows: bfloat16 [8192, 1536], P(('seq', 'head')), may hold values from -72 to 72
- image_key_rows: bfloat16 [8192, 1536], P(('seq', 'head')), may hold values from -4 to 4
- image_value_codes: int32 [8192, 1536], P(('seq', 'head')), may hold values from -127 to 127
- value_fraction: bfloat16 [8192, 1536], P(('seq', 'head')), may hold values from -0.5 to 0.5
- value_step_sizes: float32 [8, 12], replicated, may hold values from 0.004 to 0.03
- timestep_group: int32 [1000], replicated, may hold values from 0 to 7
- timestep: int32 [1], replicated, may hold values from 0 to 999
- image_output_grad: bfloat16 [8192, 1536], P(('seq', 'head')), may hold values from -1960 to 1960
- text_query_rows: bfloat16 [512, 1536], P(None, 'head'), may hold values from -4 to 4
- text_key_rows: bfloat16 [512, 1536], P(None, 'head'), may hold values from -4 to 4
- text_value_rows: bfloat16 [512, 1536], P(None, 'head'), may hold values from -4 to 4
- text_output_grad: bfloat16 [512, 1536], P(None, 'head'), may hold values from -512 to 512
Outputs:
- dq_img: bfloat16 [8192, 1536], P(('seq', 'head'))
- dk_img: bfloat16 [8192, 1536], P(('seq', 'head'))
- image_value_grad: bfloat16 [8192, 1536], P(('seq', 'head'))
- dq_txt: bfloat16 [512, 1536], P('seq', 'head')
- dk_txt: bfloat16 [512, 1536], P('seq', 'head')
- dv_txt: bfloat16 [512, 1536], P('seq', 'head')
- grad_down: float32 [3072, 64], replicated
- grad_up: float32 [64, 1536], replicated
- grad_steps: float32 [8, 12], replicated
All inputs are finite; a program needn't handle non-finite values.
Results may differ from a plain program's by a relative error of at most 0.013.
Values may be sent and summed in bfloat16 or wider, within the bound.
No kernel may reach another device: no remote copies, remote signals or barrier semaphores. Data moves between devices by JAX's collectives and lax.ppermute only.
A program may use at most 128 MiB of HBM per device.

v0:
```python
import math

import jax
import jax.numpy as jnp
from jax import lax
from jax.sharding import PartitionSpec as P

HEAD_SIZE = 128
QMAX = 127


unscale = 0.0078125


def split_heads(rows):
    return rows.reshape(rows.shape[0], rows.shape[1] // HEAD_SIZE, HEAD_SIZE)


def join_heads(heads):
    return heads.reshape(heads.shape[0], heads.shape[1] * heads.shape[2])


def head_scores(queries, key_rows):
    return jnp.einsum(
        "qhd,khd->hqk", queries, key_rows, preferred_element_type=jnp.float32
    ) * HEAD_SIZE ** (-0.5)


def over_keys(step_fn, initial, key_rows, value_rows):
    block_rows = math.gcd(key_rows.shape[0], 2048)

    def over_one_turn(turn_index, carried):
        key_block = lax.dynamic_slice_in_dim(key_rows, turn_index * block_rows, block_rows, 0)
        value_block = lax.dynamic_slice_in_dim(value_rows, turn_index * block_rows, block_rows, 0)
        return step_fn(carried, key_block, value_block)

    return lax.fori_loop(0, key_rows.shape[0] // block_rows, over_one_turn, initial)


def key_terms(carried, queries, grads, log_rows, delta_rows, own_keys, own_values):
    key_grad, value_grad = carried
    probs = jnp.exp(head_scores(queries, own_keys) - log_rows.T[:, :, None])
    dprobs = jnp.einsum("qhd,khd->hqk", grads, own_values, preferred_element_type=jnp.float32)
    dscores = (probs * (dprobs - delta_rows.T[:, :, None])).astype(jnp.bfloat16)
    value_grad = value_grad + jnp.einsum(
        "hqk,qhd->khd", probs.astype(jnp.bfloat16), grads, preferred_element_type=jnp.float32
    )
    key_grad = key_grad + jnp.einsum(
        "hqk,qhd->khd", dscores, queries, preferred_element_type=jnp.float32
    ) * HEAD_SIZE ** (-0.5)
    return (key_grad, value_grad)


def on_device(
    image_input_rows,
    adapter_down_weight,
    adapter_up_weight,
    image_query_rows,
    image_key_rows,
    image_value_codes,
    value_fraction,
    value_step_sizes,
    timestep_group,
    timestep,
    image_output_grad,
    text_query_rows,
    text_key_rows,
    text_value_rows,
    text_output_grad,
):
    slot_index = jnp.sum(
        jnp.where(
            jnp.arange(timestep_group.shape[0], dtype=jnp.int32) == timestep[0], timestep_group, 0
        )
    )
    slot_rows = jnp.arange(value_step_sizes.shape[0], dtype=jnp.int32) == slot_index
    step_row = jnp.sum(jnp.where(slot_rows[:, None], value_step_sizes, 0.0), axis=0)
    code_values = image_value_codes.astype(jnp.float32)
    v_dequant = (code_values * jnp.repeat(step_row, HEAD_SIZE)[None, :]).astype(jnp.bfloat16)
    inside = jnp.abs(image_value_codes) < QMAX
    lsq_term = jnp.where(inside, -value_fraction.astype(jnp.float32), code_values)
    query_img, key_img, value_img, grad_img = (
        lax.all_to_all(image_query_rows, "head", split_axis=1, concat_axis=0, tiled=True),
        lax.all_to_all(image_key_rows, "head", split_axis=1, concat_axis=0, tiled=True),
        lax.all_to_all(v_dequant, "head", split_axis=1, concat_axis=0, tiled=True),
        lax.all_to_all(image_output_grad, "head", split_axis=1, concat_axis=0, tiled=True),
    )
    share_rows = text_query_rows.shape[0] // lax.axis_size("seq")
    first_row = lax.axis_index("seq") * share_rows

    def own_rows(table):
        return lax.dynamic_slice_in_dim(table, first_row, share_rows, 0)

    image_rows = query_img.shape[0]
    query_local = jnp.concatenate([query_img, own_rows(text_query_rows)], axis=0)
    grad_local = jnp.concatenate([grad_img, own_rows(text_output_grad)], axis=0)
    query_split = split_heads(query_local)
    grad_split = split_heads(grad_local)
    local_count = query_split.shape[0]
    head_count = query_split.shape[1]
    key_image, value_image = (
        lax.all_gather(key_img, "seq", axis=0, tiled=True),
        lax.all_gather(value_img, "seq", axis=0, tiled=True),
    )
    text_keys = split_heads(text_key_rows)
    text_values = split_heads(text_value_rows)
    key_sets = ((split_heads(key_image), split_heads(value_image)), (text_keys, text_values))

    def stat_turn(carried, key_block, value_block):
        row_max, running, weighted = carried
        scores = head_scores(query_split, key_block)
        dprobs = jnp.einsum(
            "qhd,khd->hqk", grad_split, value_block, preferred_element_type=jnp.float32
        )
        new_max = jnp.maximum(row_max, jnp.max(scores, axis=2, keepdims=True))
        factor = jnp.exp(row_max - new_max)
        expo = jnp.exp(scores - new_max)
        running = running * factor + jnp.sum(expo, axis=2, keepdims=True)
        weighted = weighted * factor + jnp.sum(expo * dprobs, axis=2, keepdims=True)
        return (new_max, running, weighted)

    row_stats = (
        jnp.full((head_count, local_count, 1), -jnp.inf, jnp.float32),
        jnp.zeros((head_count, local_count, 1), jnp.float32),
        jnp.zeros((head_count, local_count, 1), jnp.float32),
    )
    for key_rows, value_rows in key_sets:
        row_stats = over_keys(stat_turn, row_stats, key_rows, value_rows)
    log_sums = row_stats[0] + jnp.log(row_stats[1])
    deltas = row_stats[2] / row_stats[1]

    def query_turn(running, key_block, value_block):
        probs = jnp.exp(head_scores(query_split, key_block) - log_sums)
        dprobs = jnp.einsum(
            "qhd,khd->hqk", grad_split, value_block, preferred_element_type=jnp.float32
        )
        dscores = (probs * (dprobs - deltas)).astype(jnp.bfloat16)
        return running + jnp.einsum(
            "hqk,khd->qhd", dscores, key_block, preferred_element_type=jnp.float32
        ) * HEAD_SIZE ** (-0.5)

    query_grad = jnp.zeros((local_count, head_count, HEAD_SIZE), jnp.float32)
    for key_rows, value_rows in key_sets:
        query_grad = over_keys(query_turn, query_grad, key_rows, value_rows)
    query_grad = join_heads(query_grad).astype(jnp.bfloat16)
    log_rows = log_sums[:, :, 0].T
    delta_rows = deltas[:, :, 0].T
    own_keys = split_heads(key_img)
    own_values = split_heads(value_img)
    empty = jnp.zeros(own_keys.shape, jnp.float32)
    query_rows = lax.all_gather(query_local.astype(jnp.float32), "seq", axis=0, tiled=True).astype(
        jnp.bfloat16
    )
    grad_rows = lax.all_gather(grad_local.astype(jnp.float32), "seq", axis=0, tiled=True).astype(
        jnp.bfloat16
    )
    log_part = lax.all_gather(log_rows, "seq", axis=0, tiled=True)
    delta_part = lax.all_gather(delta_rows, "seq", axis=0, tiled=True)
    piece_rows = query_rows.shape[0]
    block_rows = math.gcd(piece_rows, 2048)

    def fold_one_turn(turn_index, running):

        def rows_of(table):
            return lax.dynamic_slice_in_dim(table, turn_index * block_rows, block_rows, 0)

        return key_terms(
            running,
            split_heads(rows_of(query_rows)),
            split_heads(rows_of(grad_rows)),
            rows_of(log_part),
            rows_of(delta_part),
            own_keys,
            own_values,
        )

    key_grad, value_grad = lax.fori_loop(0, piece_rows // block_rows, fold_one_turn, (empty, empty))
    key_grad = join_heads(key_grad).astype(jnp.bfloat16)
    value_grad = join_heads(value_grad).astype(jnp.bfloat16)
    text_empty = jnp.zeros(text_keys.shape, jnp.float32)
    text_key, text_value = key_terms(
        (text_empty, text_empty),
        query_split,
        grad_split,
        log_rows,
        delta_rows,
        text_keys,
        text_values,
    )
    text_key, text_value = (
        lax.psum_scatter(join_heads(text_key), "seq", scatter_dimension=0, tiled=True),
        lax.psum_scatter(join_heads(text_value), "seq", scatter_dimension=0, tiled=True),
    )
    dk_txt = text_key.astype(jnp.bfloat16)
    dv_txt = text_value.astype(jnp.bfloat16)
    dq_txt = query_grad[image_rows:]
    dq_heads = query_grad[:image_rows]
    dq_img, dk_img, dv_quant = (
        lax.all_to_all(dq_heads, "head", split_axis=0, concat_axis=1, tiled=True),
        lax.all_to_all(key_grad, "head", split_axis=0, concat_axis=1, tiled=True),
        lax.all_to_all(value_grad, "head", split_axis=0, concat_axis=1, tiled=True),
    )
    image_value_grad = jnp.where(inside, dv_quant, jnp.zeros_like(dv_quant))
    lowrank_gradient = jnp.einsum(
        "vg,zg->vz", image_value_grad, adapter_up_weight, preferred_element_type=jnp.float32
    ).astype(jnp.bfloat16)
    part_down = jnp.einsum(
        "td,tr->dr", image_input_rows, lowrank_gradient, preferred_element_type=jnp.float32
    )
    lowrank_input = jnp.dot(
        image_input_rows, adapter_down_weight, preferred_element_type=jnp.float32
    ).astype(jnp.bfloat16)
    part_up = jnp.einsum(
        "tr,tw->rw", lowrank_input, image_value_grad, preferred_element_type=jnp.float32
    )
    token_rows = dv_quant.shape[0]
    token_terms = (dv_quant.astype(jnp.float32) * lsq_term).reshape(
        token_rows, value_step_sizes.shape[1], HEAD_SIZE
    )
    total_down, total_up, step_sums = lax.psum(
        (part_down, part_up, jnp.sum(token_terms, axis=(0, 2))), ("seq", "head")
    )
    grad_steps = jnp.where(slot_rows[:, None], step_sums[None, :], 0.0) * (QMAX ** (-0.5) * unscale)
    return (
        dq_img,
        dk_img,
        image_value_grad,
        dq_txt,
        dk_txt,
        dv_txt,
        total_down * unscale,
        total_up * unscale,
        grad_steps,
    )


def solution(mesh):
    placed = (
        P(("seq", "head"), None),
        P(),
        P(),
        P(("seq", "head"), None),
        P(("seq", "head"), None),
        P(("seq", "head"), None),
        P(("seq", "head"), None),
        P(),
        P(),
        P(),
        P(("seq", "head"), None),
        P(None, "head"),
        P(None, "head"),
        P(None, "head"),
        P(None, "head"),
    )
    return jax.shard_map(
        on_device,
        mesh=mesh,
        in_specs=placed,
        out_specs=(
            P(("seq", "head"), None),
            P(("seq", "head"), None),
            P(("seq", "head"), None),
            P("seq", "head"),
            P("seq", "head"),
            P("seq", "head"),
            P(),
            P(),
            P(),
        ),
        check_vma=False,
    )
```

profile of v0, /device:TPU:1, one launch (start us, length us, event | category | flops | bytes accessed | tf_op | source)
XLA Modules:
  0.0 793.6 jit_solution(15537787411285271635)
XLA Ops:
  8.2 9.6 %all_to_all.127 = bf16[32,4,384]{2,0,1:T(8,128)(2,1)} all-to-all(bf16[32,4,384]{2,0,1:T(8,128)(2,1)S(1)} %bitcast.239), channel_id=1, replica_groups=mesh['seq'=64,'head'=4] {'head'}, dimensions={1} | all-to-all | bytes 196608 | tf_op jit(solution)/shard_map/all_to_all | solution.py:84
  18.5 1.3 select_reduce_fusion.1
  22.3 7.7 all_to_all.128
  30.1 1.6 copy.257
  31.6 3.3 all-to-all-start.1
  35.7 3.9 all-to-all-done.1
  40.3 1.5 copy.255
  41.8 3.3 all-to-all-start.3
  45.9 3.9 all-to-all-done.3
  55.2 46.7 %all-gather.7.cloned.1.call-done = bf16[8192,384]{1,0:T(8,128)(2,1)} async-done(((bf16[128,384]{1,0:T(8,128)(2,1)}), bf16[8192,384]{1,0:T(8,128)(2,1)}) %all-gather.7.cloned.1.call-update) | async-done | bytes 6291472 | tf_op jit(solution)/shard_map/all_gather | solution.py:102
  101.9 8.7 %copy.207 = bf16[8192,384]{0,1:T(8,128)(2,1)} copy(bf16[8192,384]{1,0:T(8,128)(2,1)} %all-gather.7.cloned.1.call-done) | data formatting | bytes 12582912 | tf_op jit(solution)/shard_map/all_gather | solution.py:102
  110.6 8.7 %copy.220 = bf16[8192,3,128]{2,0,1:T(8,128)(2,1)} copy(bf16[8192,3,128]{0,2,1:T(8,128)(2,1)} %bitcast.217) | data formatting | bytes 12582912
  119.3 63.1 %all-gather.9.cloned.1.call-done = bf16[8192,384]{1,0:T(8,128)(2,1)} async-done(((bf16[128,384]{1,0:T(8,128)(2,1)}), bf16[8192,384]{1,0:T(8,128)(2,1)}) %all-gather.9.cloned.1.call-update) | async-done | bytes 6291472 | tf_op jit(solution)/shard_map/all_gather | solution.py:103
  182.4 8.7 %copy.211 = bf16[8192,384]{0,1:T(8,128)(2,1)} copy(bf16[8192,384]{1,0:T(8,128)(2,1)} %all-gather.9.cloned.1.call-done) | data formatting | bytes 12582912 | tf_op jit(solution)/shard_map/all_gather | solution.py:103
  191.1 8.7 %copy.215 = bf16[8192,3,128]{2,0,1:T(8,128)(2,1)} copy(bf16[8192,3,128]{0,2,1:T(8,128)(2,1)} %bitcast.218) | data formatting | bytes 12582912
  199.8 35.9 %while.60 = (s32[]{:T(128)}, f32[3,136,1]{1,0,2:T(4,128)S(1)}, f32[3,136,1]{1,0,2:T(4,128)S(1)}, f32[3,136,1]{1,0,2:T(4,128)S(1)}, bf16[8192,3,128]{2,0,1:T(8,12...) while((s32[]{:T(128)}, f32[3,136,1]{1,0,2:T(4,128)S(1)}, ...), condition=%wide.region_6.7_spmd.clone, body=%wide.region_2.6_spmd.clone.sunk | while | flops 435342112 | bytes 26780568 | solution.py:37
  199.8 4.3 bitcast_reduce_fusion.3
  204.0 3.9 fusion.107
  208.7 4.3 bitcast_reduce_fusion.3
  213.0 3.9 fusion.107
  217.7 4.3 bitcast_reduce_fusion.3
  222.0 3.9 fusion.107
  226.7 4.3 bitcast_reduce_fusion.3
  231.0 3.9 fusion.107
  236.8 42.9 %all-gather = f32[64,136,3]{1,2,0:T(4,128)S(1)} all-gather(f32[1,136,3]{1,2,0:T(4,128)S(1)} %bitcast.246), channel_id=1, replica_groups=mesh['seq'=64,'head'=4] {'seq'}, dimensions={0}, use_global_device_ids=true | all-gather | bytes 106080 | tf_op jit(solution)/shard_map/all_gather | solution.py:157
  280.0 42.6 %all-gather.1 = f32[64,136,3]{1,2,0:T(4,128)S(1)} all-gather(f32[1,136,3]{1,2,0:T(4,128)S(1)} %bitcast.250), channel_id=1, replica_groups=mesh['seq'=64,'head'=4] {'seq'}, dimensions={0}, use_global_device_ids=true | all-gather | bytes 106080 | tf_op jit(solution)/shard_map/all_gather | solution.py:158
  322.9 1.4 multiply_convert_fusion.1
  324.3 38.4 %while.61 = (s32[]{:T(128)}, f32[136,3,128]{2,0,1:T(8,128)}, bf16[8192,3,128]{2,0,1:T(8,128)(2,1)}, bf16[136,3,128]{2,0,1:T(8,128)(2,1)S(1)}, f32[3,136,1]{1,0,2...) while((s32[]{:T(128)}, f32[136,3,128]{2,0,1:T(8,128)}, ...), condition=%wide.region_11.12_spmd.clone, body=%wide.region_10.11_spmd.clone.sunk | while | flops 646063104 | bytes 12034936 | solution.py:37
  324.3 4.3 fusion.114
  328.6 5.4 fusion.115
  334.0 4.3 fusion.114
  338.3 5.3 fusion.115
  343.6 4.3 fusion.114
  347.8 5.3 fusion.115
  353.2 4.3 fusion.114
  357.4 5.3 fusion.115
  362.7 1.8 fusion.47
  364.6 1.2 convolution_multiply_fusion.2
  365.8 1.3 fusion.51
  367.1 50.0 %while.62 = (s32[]{:T(128)}, f32[128,3,128]{0,2,1:T(8,128)S(1)}, f32[128,3,128]{0,2,1:T(8,128)S(1)}, bf16[8704,384]{1,0:T(8,128)(2,1)}, bf16[128,3,128]{2,0,1:T(...) while((s32[]{:T(128)}, f32[128,3,128]{0,2,1:T(8,128)S(1)}, ...), condition=%wide.region_13.14_spmd.clone, body=%wide.region_12.13_spmd.clone.sunk | while | flops 202752000 | bytes 8097990 | solution.py:177
  370.0 1.2 constant_dynamic-slice_fusion.5
  373.0 1.2 constant_dynamic-slice_fusion.5
  375.9 1.2 constant_dynamic-slice_fusion.5
  378.9 1.2 constant_dynamic-slice_fusion.5
  381.8 1.2 constant_dynamic-slice_fusion.5
  384.7 1.2 constant_dynamic-slice_fusion.5
  387.7 1.2 constant_dynamic-slice_fusion.5
  390.6 1.2 constant_dynamic-slice_fusion.5
  393.6 1.2 constant_dynamic-slice_fusion.5
  396.5 1.2 constant_dynamic-slice_fusion.5
  399.4 1.2 constant_dynamic-slice_fusion.5
  402.4 1.2 constant_dynamic-slice_fusion.5
  418.0 3.9 all-to-all-start.6
  421.9 1.3 slice_bitcast_fusion
  424.9 1.4 copy.235
  426.6 4.3 all-to-all-start.4
  432.0 2.5 convolution_bitcast_fusion.1
  434.5 1.3 fusion.48
  435.8 259.4 %all-reduce.8 = (bf16[512,384]{1,0:T(8,128)(2,1)S(1)}, bf16[512,384]{1,0:T(8,128)(2,1)}) all-reduce(f32[512,384]{1,0:T(8,128)S(1)} %copy.235, f32[512,384]{1,0:T(8,128)S(1)} %copy.236), channel_id=2, replica_groups=mesh['seq'=64,'head'=4] {'seq'}, use_global_device_ids=true, to_apply=%region_14.15.clone | all-reduce | flops 393216 | bytes 2359296
  695.2 1.3 dynamic-slice_convert_fusion
  697.5 4.1 all-to-all-start.5
  702.4 79.6 %psum.23 = f32[12]{0:T(128)S(1)} all-reduce(f32[12]{0:T(128)S(1)} %bitcast_reduce_fusion.1), channel_id=1, replica_groups=mesh['seq'=64,'head'=4] {'seq','head'}, use_global_device_ids=true, to_apply=%region_20.21 | all-reduce | flops 12 | bytes 96 | tf_op jit(solution)/shard_map/psum | solution.py:220
  783.3 2.1 broadcast_multiply_fusion
  785.3 1.8 broadcast_multiply_fusion.1
  (223 shorter events, 56.3 us)
Async XLA Ops:
  7.2 427.3 %copy-start = (bf16[3072,64]{0,1:T(8,128)(2,1)S(1)}, bf16[3072,64]{0,1:T(8,128)(2,1)}, u32[]{:S(2)}) copy-start(bf16[3072,64]{0,1:T(8,128)(2,1)} %param.22) | copy-start | bytes 1179652
  7.2 44.7 %copy-start.10 = (u32[256]{0:T(256)S(1)}, u32[256]{0:T(256)}, u32[]{:S(2)}) copy-start(u32[256]{0:T(256)} %constant.179) | copy-start | bytes 3076
  7.2 44.4 %copy-start.8 = (bf16[512,384]{1,0:T(8,128)(2,1)S(1)}, bf16[512,384]{1,0:T(8,128)(2,1)}, u32[]{:S(2)}) copy-start(bf16[512,384]{1,0:T(8,128)(2,1)} %param.34) | copy-start | bytes 1179652
  7.2 94.7 %all-gather.7.cloned.1.call-start = ((), (), s32[]{:S(2)}) async-start(), calls=%async_computation.7 | async-start | bytes 6389760 | tf_op jit(solution)/shard_map/all_gather | solution.py:102
  17.8 36.8 %copy-start.4 = (bf16[32,4,384]{2,0,1:T(8,128)(2,1)S(1)}, bf16[32,4,384]{2,0,1:T(8,128)(2,1)}, u32[]{:S(2)}) copy-start(bf16[32,4,384]{2,0,1:T(8,128)(2,1)} %all_to_all.127) | copy-start | bytes 294916
  17.8 164.5 %all-gather.9.cloned.1.call-start = ((), (), s32[]{:S(2)}) async-start(), calls=%async_computation.8 | async-start | bytes 6389760 | tf_op jit(solution)/shard_map/all_gather | solution.py:103
  30.0 24.7 %copy-start.5 = (bf16[32,4,384]{2,0,1:T(8,128)(2,1)S(1)}, bf16[32,4,384]{2,0,1:T(8,128)(2,1)}, u32[]{:S(2)}) copy-start(bf16[32,4,384]{2,0,1:T(8,128)(2,1)} %all_to_all.128) | copy-start | bytes 294916
  31.6 7.9 all-to-all-start.1
  35.0 332.2 %all-gather.11.cloned.1.call-start = ((), (), s32[]{:S(2)}) async-start(), calls=%async_computation.9 | async-start | bytes 6789120 | tf_op jit(solution)/shard_map/all_gather | solution.py:151
  41.8 7.9 all-to-all-start.3
  45.1 322.0 %all-gather.13.cloned.1.call-start = ((), (), s32[]{:S(2)}) async-start(), calls=%async_computation.10 | async-start | bytes 6789120 | tf_op jit(solution)/shard_map/all_gather | solution.py:154
  204.0 3.9 copy-start.1
  213.0 3.9 copy-start.1
  222.0 3.9 copy-start.1
  231.0 3.9 copy-start.1
  417.1 9.3 %copy-start.2 = (f32[3,128,512]{2,1,0:T(8,128)S(1)}, f32[3,128,512]{2,1,0:T(8,128)}, u32[]{:S(2)}) copy-start(f32[3,128,512]{2,1,0:T(8,128)} %fusion.51) | copy-start | bytes 2359300
  417.1 14.8 %copy-start.3 = (s32[32,1536]{1,0:T(8,128)S(1)}, s32[32,1536]{1,0:T(8,128)}, u32[]{:S(2)}) copy-start(s32[32,1536]{1,0:T(8,128)} %param.26) | copy-start | bytes 589828
  417.1 17.3 %copy-start.7 = (bf16[32,3072]{1,0:T(8,128)(2,1)S(1)}, bf16[32,3072]{1,0:T(8,128)(2,1)}, u32[]{:S(2)}) copy-start(bf16[32,3072]{1,0:T(8,128)(2,1)} %param.21) | copy-start | bytes 589828
  418.0 8.6 %all-to-all-start.6 = ((bf16[4,32,384]{2,1,0:T(8,128)(2,1)}), bf16[4,32,384]{2,1,0:T(8,128)(2,1)}, u32[]{:S(2)}, u32[]{:S(2)}) async-start(bf16[4,32,384]{2,1,0:T(8,128)(2,1)} %convert_element_type.92), calls=%async_computation.6 | async-start | bytes 196608 | tf_op jit(solution)/shard_map/all_to_all | solution.py:201
  426.6 270.7 %copy-start.9 = (bf16[32,1536]{1,0:T(8,128)(2,1)S(1)}, bf16[32,1536]{1,0:T(8,128)(2,1)}, u32[]{:S(2)}) copy-start(bf16[32,1536]{1,0:T(8,128)(2,1)} %param.27) | copy-start | bytes 294916
  426.6 270.8 %all-to-all-start.4 = ((bf16[4,32,384]{2,1,0:T(8,128)(2,1)}), bf16[4,32,384]{2,1,0:T(8,128)(2,1)S(1)}, u32[]{:S(2)}, u32[]{:S(2)}) async-start(bf16[4,32,384]{2,1,0:T(8,128)(2,1)} %all_to_all.108), calls=%async_computation.4 | async-start | bytes 196608 | tf_op jit(solution)/shard_map/all_to_all | solution.py:199
  431.0 352.3 %all-reduce.7.cloned.1.call-start = ((), (), s32[]{:S(2)}) async-start(), calls=%async_computation.11 | async-start | bytes 2359296 | tf_op jit(solution)/shard_map/psum | solution.py:220
  432.0 270.4 %copy-start.6 = (bf16[32,1536]{1,0:T(8,128)(2,1)}, bf16[32,1536]{1,0:T(8,128)(2,1)S(1)}, u32[]{:S(2)}) copy-start(bf16[32,1536]{1,0:T(8,128)(2,1)S(1)} %fusion.54) | copy-start | bytes 294916
  697.5 84.5 %all-to-all-start.5 = ((bf16[4,32,384]{2,1,0:T(8,128)(2,1)}), bf16[4,32,384]{2,1,0:T(8,128)(2,1)S(1)}, u32[]{:S(2)}, u32[]{:S(2)}) async-start(bf16[4,32,384]{2,1,0:T(8,128)(2,1)} %convert_element_type.90), calls=%async_computation.5 | async-start | bytes 196608 | tf_op jit(solution)/shard_map/all_to_all | solution.py:200
Sparse Core Ops, SparseCore 0:
  18.0 83.8 all-gather.6
  104.6 77.6 all-gather.8
  185.1 78.0 all-gather.10
  265.9 78.0 all-gather.12
  437.5 255.5 all-reduce.6
where the time goes:
time: 797 us; the launch traced here: 794 us
  blocking collectives  442 us (55%)
  waiting for transfers between devices  118 us (15%)
  matrix products  103 us (13%)
  local copies, waits for them, and re-layouts  81.5 us (10%)
  starting transfers between devices  19.1 us (2%)
  between operations  15.5 us (2%)
  other arithmetic  14.2 us (2%)
    unnamed x1, blocking collectives  259 us
    psum x1, blocking collectives, on_device(): lax.psum((part_down, part_up, jnp.sum(token_terms, axis=(0, 2))), ('seq',...  79.6 us
    all_gather x1, waiting for transfers between devices, on_device(): lax.all_gather(value_img, 'seq', axis=0, tiled=True)  63.1 us
    all_gather x1, waiting for transfers between devices, on_device(): lax.all_gather(key_img, 'seq', axis=0, tiled=True)  46.7 us
    all_gather x1, blocking collectives, on_device(): log_part = lax.all_gather(log_rows, 'seq', axis=0, tiled=True)  42.9 us
    all_gather x1, blocking collectives, on_device(): delta_part = lax.all_gather(delta_rows, 'seq', axis=0, tiled=True)  42.6 us
    dot_general x26, matrix products, head_scores(): jnp.einsum('qhd,khd->hqk', queries, key_rows, preferred_element_type=jnp....  41.6 us
    dynamic_slice x51, local copies, waits for them, and re-layouts, rows_of(): lax.dynamic_slice_in_dim(table, turn_index * block_rows, block_rows, 0)  26.8 us
  transfers between devices with their start and end apart: 10, of which 4 were waited for; matrix products, arithmetic and copies ran while one was open for 18% of the time, Pallas kernels for 0%

commit v1 on v0

v1 whole, which is shorter than its diff:
```python
import functools
import math

import jax
import jax.numpy as jnp
from jax import lax
from jax.experimental import pallas as pl
from jax.experimental.pallas import tpu as pltpu
from jax.sharding import Mesh
from jax.sharding import PartitionSpec as P

HEAD_SIZE = 128
QMAX = 127
UNSCALE = 0.0078125
SCALE = HEAD_SIZE ** -0.5
SCALE_LOG2 = SCALE * math.log2(math.e)

IMG_ROWS = 1024
TXT_ROWS = 64
ROWS = IMG_ROWS + TXT_ROWS
HEADS = 3
TILE = 512

BF16 = jnp.bfloat16
F32 = jnp.float32
NT = (((1,), (1,)), ((), ()))
NN = (((1,), (0,)), ((), ()))
TN = (((0,), (0,)), ((), ()))


def dot(a, b, dims):
    return lax.dot_general(a, b, dims, preferred_element_type=F32)


def query_tiles():
    return [(s, TILE) for s in range(0, IMG_ROWS, TILE)] + [(IMG_ROWS, TXT_ROWS)]


def load_rows(scratch, gathered, which, text):
    scratch[0:IMG_ROWS] = gathered[:, which].reshape(IMG_ROWS, HEAD_SIZE)
    scratch[IMG_ROWS:ROWS] = text[...]


def stat_kernel(gq, gk, qt, gt, kt, vt, out, k_s, v_s, q_s, g_s):
    h = pl.program_id(0)
    load_rows(k_s, gk, 0, kt)
    load_rows(v_s, gk, 1, vt)
    load_rows(q_s, gq, 0, qt)
    load_rows(g_s, gq, 1, gt)
    for s, n in query_tiles():
        st = dot(k_s[...], q_s[s:s + n], NT)
        m = jnp.max(st, axis=0, keepdims=True)
        e = jnp.exp2((st - m) * SCALE_LOG2)
        l = jnp.sum(e, axis=0, keepdims=True)
        dp = dot(v_s[...], g_s[s:s + n], NT)
        w = jnp.sum(e * dp, axis=0, keepdims=True)
        log_sum = m * SCALE_LOG2 + jnp.log2(l)
        delta = w / l
        rows = lax.broadcasted_iota(jnp.int32, (8, n), 0)
        old = jnp.where(h == 0, 0.0, out[:, s:s + n])
        out[:, s:s + n] = jnp.where(
            rows == 2 * h, log_sum, jnp.where(rows == 2 * h + 1, delta, old)
        )


def grad_kernel(gq, gk, qt, gt, kt, vt, stats, dq, dkv, k_s, v_s, q_s, g_s, p_s, d_s, st_s):
    h = pl.program_id(0)
    load_rows(k_s, gk, 0, kt)
    load_rows(v_s, gk, 1, vt)
    load_rows(q_s, gq, 0, qt)
    load_rows(g_s, gq, 1, gt)
    logs = stats[:, pl.ds(2 * h, 1), :]
    deltas = stats[:, pl.ds(2 * h + 1, 1), :]
    m = jnp.max(logs, axis=0)
    e = jnp.exp2(logs - m[None])
    l = jnp.sum(e, axis=0)
    st_s[0:1] = m + jnp.log2(l)
    st_s[1:2] = jnp.sum(e * deltas, axis=0) / l
    for s, n in query_tiles():
        st = dot(k_s[...], q_s[s:s + n], NT)
        p = jnp.exp2(st * SCALE_LOG2 - st_s[0:1, s:s + n])
        dp = dot(v_s[...], g_s[s:s + n], NT)
        ds = p * (dp - st_s[1:2, s:s + n])
        p_s[:, s:s + n] = p.astype(BF16)
        d_s[:, s:s + n] = ds.astype(BF16)
    dv = dot(p_s[...], g_s[...], NN)
    dk = dot(d_s[...], q_s[...], NN) * SCALE
    dqv = dot(d_s[...], k_s[...], TN) * SCALE
    blank = jnp.zeros((8, 8, HEAD_SIZE), F32)
    dkv[:, 0:128] = dk[:IMG_ROWS].astype(BF16).reshape(8, 128, HEAD_SIZE)
    dkv[:, 128:256] = dv[:IMG_ROWS].astype(BF16).reshape(8, 128, HEAD_SIZE)
    dkv[:, 256:272] = jnp.concatenate(
        [dk[IMG_ROWS:].reshape(8, 8, HEAD_SIZE), dv[IMG_ROWS:].reshape(8, 8, HEAD_SIZE)], axis=1
    ).astype(BF16)
    dq[:, 0:128] = dqv[:IMG_ROWS].astype(BF16).reshape(8, 128, HEAD_SIZE)
    dq[:, 128:144] = jnp.concatenate(
        [dqv[IMG_ROWS:].reshape(8, 8, HEAD_SIZE), blank], axis=1
    ).astype(BF16)


def row_specs():
    image = pl.BlockSpec((32, 2, 32, HEAD_SIZE), lambda h: (0, 0, 0, h))
    text = pl.BlockSpec((TXT_ROWS, HEAD_SIZE), lambda h: (0, h))
    return [image, image, text, text, text, text]


def row_scratch():
    return [pltpu.VMEM((ROWS, HEAD_SIZE), BF16)] * 4


def row_stats(*rows):
    return pl.pallas_call(
        stat_kernel,
        grid=(HEADS,),
        in_specs=row_specs(),
        out_specs=pl.BlockSpec((8, ROWS), lambda h: (0, 0)),
        out_shape=jax.ShapeDtypeStruct((8, ROWS), F32),
        scratch_shapes=row_scratch(),
        name="row_stats",
        compiler_params=pltpu.CompilerParams(vmem_limit_bytes=48 << 20),
        cost_estimate=pl.CostEstimate(
            flops=4 * HEADS * ROWS * ROWS * HEAD_SIZE,
            bytes_accessed=4 << 20,
            transcendentals=HEADS * ROWS * ROWS,
        ),
    )(*rows)


def row_grads(*operands):
    return pl.pallas_call(
        grad_kernel,
        grid=(HEADS,),
        in_specs=row_specs() + [pl.BlockSpec((8, 8, ROWS), lambda h: (0, 0, 0))],
        out_specs=[
            pl.BlockSpec((8, 144, HEAD_SIZE), lambda h: (0, 0, h)),
            pl.BlockSpec((8, 272, HEAD_SIZE), lambda h: (0, 0, h)),
        ],
        out_shape=[
            jax.ShapeDtypeStruct((8, 144, HEADS * HEAD_SIZE), BF16),
            jax.ShapeDtypeStruct((8, 272, HEADS * HEAD_SIZE), BF16),
        ],
        scratch_shapes=row_scratch()
        + [pltpu.VMEM((ROWS, ROWS), BF16)] * 2
        + [pltpu.VMEM((8, ROWS), F32)],
        name="row_grads",
        compiler_params=pltpu.CompilerParams(vmem_limit_bytes=56 << 20),
        cost_estimate=pl.CostEstimate(
            flops=10 * HEADS * ROWS * ROWS * HEAD_SIZE,
            bytes_accessed=8 << 20,
            transcendentals=HEADS * ROWS * ROWS,
        ),
    )(*operands)


def on_device(
    image_input_rows,
    adapter_down_weight,
    adapter_up_weight,
    image_query_rows,
    image_key_rows,
    image_value_codes,
    value_fraction,
    value_step_sizes,
    timestep_group,
    timestep,
    image_output_grad,
    text_query_rows,
    text_key_rows,
    text_value_rows,
    text_output_grad,
):
    slot_index = jnp.sum(
        jnp.where(
            jnp.arange(timestep_group.shape[0], dtype=jnp.int32) == timestep[0], timestep_group, 0
        )
    )
    slot_rows = jnp.arange(value_step_sizes.shape[0], dtype=jnp.int32) == slot_index
    step_row = jnp.sum(jnp.where(slot_rows[:, None], value_step_sizes, 0.0), axis=0)
    code_values = image_value_codes.astype(F32)
    v_dequant = (code_values * jnp.repeat(step_row, HEAD_SIZE)[None, :]).astype(BF16)
    inside = jnp.abs(image_value_codes) < QMAX
    lsq_term = jnp.where(inside, -value_fraction.astype(F32), code_values)

    groups = lax.axis_size("head")
    width = image_query_rows.shape[1] // groups

    def by_group(rows):
        return rows.reshape(rows.shape[0], groups, width).transpose(1, 0, 2)

    packed = jnp.stack(
        [
            by_group(image_query_rows),
            by_group(image_output_grad),
            by_group(image_key_rows),
            by_group(v_dequant),
        ],
        axis=1,
    )
    own = lax.all_to_all(packed, "head", split_axis=0, concat_axis=0, tiled=True)
    token_rows = image_query_rows.shape[0]

    def gather(part, axes):
        flat = part.reshape(groups * 2 * token_rows, width)
        whole = lax.all_gather(flat, axes, axis=0, tiled=True)
        return whole.reshape(-1, 2, token_rows, width)

    gq = gather(own[:, 0:2], "z")
    gk = gather(own[:, 2:4], ("x", "core"))

    x_size, z_size, core_size = lax.axis_size("x"), lax.axis_size("z"), lax.axis_size("core")
    share = text_query_rows.shape[0] // (x_size * z_size * core_size)

    def text_for_queries(rows):
        table = rows.reshape(x_size, z_size, core_size, share, width)
        table = lax.dynamic_index_in_dim(table, lax.axis_index("x"), 0, keepdims=False)
        table = lax.dynamic_index_in_dim(table, lax.axis_index("core"), 1, keepdims=False)
        return table.reshape(z_size * share, width)

    def text_for_keys(rows):
        table = rows.reshape(x_size, z_size, core_size, share, width)
        table = lax.dynamic_index_in_dim(table, lax.axis_index("z"), 1, keepdims=False)
        return table.reshape(x_size * core_size * share, width)

    rows = (
        gq,
        gk,
        text_for_queries(text_query_rows),
        text_for_queries(text_output_grad),
        text_for_keys(text_key_rows),
        text_for_keys(text_value_rows),
    )
    stats = row_stats(*rows)
    all_stats = lax.all_gather(stats, "z", axis=0)
    dq_part, dkv_part = row_grads(*rows, all_stats)

    dkv_part = lax.all_to_all(dkv_part, ("x", "core"), split_axis=0, concat_axis=0, tiled=True)
    dq_part = lax.all_to_all(dq_part, "z", split_axis=0, concat_axis=0, tiled=True)
    dkv = jnp.sum(dkv_part.astype(F32), axis=0).astype(BF16)
    dq = jnp.sum(dq_part.astype(F32), axis=0).astype(BF16)
    dq_txt = dq[128:136]
    dk_txt = dkv[256:264]
    dv_txt = dkv[264:272]
    back = jnp.stack(
        [
            dq[0:128].reshape(groups, token_rows, width),
            dkv[0:128].reshape(groups, token_rows, width),
            dkv[128:256].reshape(groups, token_rows, width),
        ],
        axis=1,
    )
    back = lax.all_to_all(back, "head", split_axis=0, concat_axis=0, tiled=True)
    back = back.transpose(1, 2, 0, 3).reshape(3, token_rows, groups * width)
    dq_img, dk_img, dv_quant = back[0], back[1], back[2]

    image_value_grad = jnp.where(inside, dv_quant, jnp.zeros_like(dv_quant))
    lowrank_gradient = jnp.einsum(
        "vg,zg->vz", image_value_grad, adapter_up_weight, preferred_element_type=F32
    ).astype(BF16)
    part_down = jnp.einsum(
        "td,tr->dr", image_input_rows, lowrank_gradient, preferred_element_type=F32
    )
    lowrank_input = jnp.dot(
        image_input_rows, adapter_down_weight, preferred_element_type=F32
    ).astype(BF16)
    part_up = jnp.einsum(
        "tr,tw->rw", lowrank_input, image_value_grad, preferred_element_type=F32
    )
    token_terms = (dv_quant.astype(F32) * lsq_term).reshape(
        token_rows, value_step_sizes.shape[1], HEAD_SIZE
    )
    total_down, total_up, step_sums = lax.psum(
        (part_down, part_up, jnp.sum(token_terms, axis=(0, 2))), ("x", "z", "core", "head")
    )
    grad_steps = jnp.where(slot_rows[:, None], step_sums[None, :], 0.0) * (QMAX ** (-0.5) * UNSCALE)
    return (
        dq_img,
        dk_img,
        image_value_grad,
        dq_txt,
        dk_txt,
        dv_txt,
        total_down * UNSCALE,
        total_up * UNSCALE,
        grad_steps,
    )


def solution(mesh):
    fine = Mesh(mesh.devices.reshape(4, 8, 2, 4), ("x", "z", "core", "head"))
    seq = ("x", "z", "core")
    tokens = P(seq + ("head",), None)
    heads = P(None, "head")
    return jax.shard_map(
        on_device,
        mesh=fine,
        in_specs=(
            tokens,
            P(),
            P(),
            tokens,
            tokens,
            tokens,
            tokens,
            P(),
            P(),
            P(),
            tokens,
            heads,
            heads,
            heads,
            heads,
        ),
        out_specs=(
            tokens,
            tokens,
            tokens,
            P(seq, "head"),
            P(seq, "head"),
            P(seq, "head"),
            P(),
            P(),
            P(),
        ),
        check_vma=False,
    )
```

time: 797 us -> 482 us (0.60)
  blocking collectives: 442 us -> 150 us
  waiting for transfers between devices: 118 us -> 268 us
  matrix products: 103 us -> 2.73 us
  local copies, waits for them, and re-layouts: 81.5 us -> 11 us
  Pallas kernels: 0 us -> 20 us
  starting transfers between devices: 19.1 us -> 5.47 us
    unnamed x1 -> x0, blocking collectives: 259 us -> none
    psum x1, waiting for transfers between devices: 0.01 us -> 174 us  [on_device(): lax.psum((part_down, part_up, jnp.sum(token_terms, axis=(0, 2))), ('x', '...]
    dot_general x72 -> x0, matrix products: 98.7 us -> none  [the longest x26 41.6 us: head_scores(): jnp.einsum('qhd,khd->hqk', queries, key_rows, preferred_element_type=jnp....]
    all_gather x2 -> x1, blocking collectives: 85.6 us -> 22.5 us  [on_device(): all_stats = lax.all_gather(stats, 'z', axis=0)]
    all_gather x4 -> x2, waiting for transfers between devices: 110 us -> 68.1 us  [gather(): whole = lax.all_gather(flat, axes, axis=0, tiled=True)]
    all_to_all x2 -> x3, blocking collectives: 17.3 us -> 53.7 us  [the longest x1 31.7 us: on_device(): lax.all_to_all(dkv_part, ('x', 'core'), split_axis=0, concat_axis=0, tile...]
    dynamic_slice x53 -> x1, local copies, waits for them, and re-layouts: 28.2 us -> 0.84 us  [text_for_keys(): lax.dynamic_index_in_dim(table, lax.axis_index('z'), 1, keepdims=False)]
    pallas_call x0 -> x2, Pallas kernels: none -> 20 us  [the longest x1 13 us: row_grads(): pl.pallas_call(grad_kernel, grid=(HEADS,), in_specs=row_specs() + [pl.Blo...]
  transfers between devices with their start and end apart: 10 -> 4, of which waited for: 4 -> 4; matrix products, arithmetic and copies ran while one was open for 18% -> 1% of each run, Pallas kernels for 0% -> 0%
where the time goes in v1:
time: 482 us; the launch traced here: 479 us
  waiting for transfers between devices  268 us (56%)
  blocking collectives  150 us (31%)
  Pallas kernels  20 us (4%)
  between operations  14.7 us (3%)
  local copies, waits for them, and re-layouts  11 us (2%)
  other arithmetic  8.3 us (2%)
  starting transfers between devices  5.47 us (1%)
    psum x1, waiting for transfers between devices, on_device(): lax.psum((part_down, part_up, jnp.sum(token_terms, axis=(0, 2))), ('x', '...  174 us
    psum x1, blocking collectives, on_device(): lax.psum((part_down, part_up, jnp.sum(token_terms, axis=(0, 2))), ('x', '...  73.3 us
    all_gather x2, waiting for transfers between devices, gather(): whole = lax.all_gather(flat, axes, axis=0, tiled=True)  68.1 us
    all_to_all x1, blocking collectives, on_device(): lax.all_to_all(dkv_part, ('x', 'core'), split_axis=0, concat_axis=0, tile...  31.7 us
    all_to_all x1, waiting for transfers between devices, on_device(): lax.all_to_all(dq_part, 'z', split_axis=0, concat_axis=0, tiled=True)  25.3 us
    all_gather x1, blocking collectives, on_device(): all_stats = lax.all_gather(stats, 'z', axis=0)  22.5 us
    pallas_call x1, Pallas kernels, row_grads(): pl.pallas_call(grad_kernel, grid=(HEADS,), in_specs=row_specs() + [pl.Blo...  13 us
    all_to_all x1, blocking collectives, on_device(): lax.all_to_all(packed, 'head', split_axis=0, concat_axis=0, tiled=True)  12 us
  transfers between devices with their start and end apart: 4, of which 4 were waited for; matrix products, arithmetic and copies ran while one was open for 1% of the time, Pallas kernels for 0%

profile of v1, /device:TPU:1, one launch (start us, length us, event | category | flops | bytes accessed | tf_op | source)
XLA Modules:
  0.0 479.4 jit_solution(17856472566561488660)
XLA Ops:
  7.2 0.0 copy-start
  7.2 0.0 all-gather.4.cloned.1.call-start
  7.9 1.3 select_reduce_fusion.1
  9.2 0.6 iota_compare_fusion.1
  9.9 0.8 select_reduce_fusion
  10.7 0.1 broadcast_bitcast_fusion
  10.8 0.9 multiply_convert_fusion
  11.7 0.9 reshape.89
  12.7 0.9 reshape.91
  13.6 0.9 reshape.90
  14.5 0.4 pad_maximum_fusion
  14.9 12.0 %all_to_all.20 = bf16[4,4,32,384]{3,2,1,0:T(8,128)(2,1)S(1)} all-to-all(bf16[4,4,32,384]{3,2,1,0:T(8,128)(2,1)S(1)} %copy.45), channel_id=1, replica_groups=mesh['x'=4,'z'=8,'core'=2,'head'=4] {'head'}, dimensions={0} | all-to-all | bytes 786432 | tf_op jit(solution)/shard_map/all_to_all | solution.py:199
  26.9 0.8 fusion.2
  27.7 0.0 all-gather.4.cloned.1.call-update
  27.7 0.0 all-gather.6.cloned.1.call-start
  27.8 0.7 all-gather.6.cloned.1.call-update
  28.5 0.8 constant_dynamic-slice_fusion
  29.3 0.0 copy-start.1
  29.3 0.0 copy-start.2
  29.3 0.9 dynamic-slice_bitcast_fusion
  30.2 0.0 copy-start.3
  30.2 0.0 copy-start.4
  30.2 35.9 %all-gather.4.cloned.1.call-done = bf16[2048,384]{1,0:T(8,128)(2,1)} async-done(((bf16[256,384]{1,0:T(8,128)(2,1)}), bf16[2048,384]{1,0:T(8,128)(2,1)}) %all-gather.4.cloned.1.call-update) | async-done | bytes 1572880 | tf_op jit(solution)/shard_map/all_gather | solution.py:204
  66.2 32.1 %all-gather.6.cloned.1.call-done = bf16[2048,384]{1,0:T(8,128)(2,1)} async-done(((bf16[256,384]{1,0:T(8,128)(2,1)}), bf16[2048,384]{1,0:T(8,128)(2,1)}) %all-gather.6.cloned.1.call-update) | async-done | bytes 1572880 | tf_op jit(solution)/shard_map/all_gather | solution.py:204
  98.3 1.4 copy-done.5
  99.7 1.4 copy-done.6
  101.1 6.9 %row_stats.1 = f32[8,1088]{1,0:T(8,128)S(1)} custom-call(bf16[32,2,32,384]{3,2,1,0:T(8,128)(2,1)S(1)} %bitcast.67, bf16[32,2,32,384]{3,2,1,0:T(8,128)(2,1)S(1)} %bitcast.69, bf16[64,384]{1,0:T(8,128)(2,1)S(1)} %get-tuple-element.25.qt, bf16[64,384]{1,0:T(8,128)(2,1)S(1)} %get-tuple-element.24.gt, bf16[64,384]{1,0:T(8,128)(2,1)S(1)} %bitcast.62, ...), custom_call_target="tpu_custom_call" | custom-call | flops 1818230784 | bytes 4194304 | tf_op jit(solution)/shard_map/row_stats/pallas_call | solution.py:112
  108.1 0.0 copy-done.1
  108.1 0.0 copy-done.2
  108.1 0.0 copy-done.3
  108.1 22.5 %all-gather = f32[64,1088]{1,0:T(8,128)} all-gather(f32[8,1088]{1,0:T(8,128)S(1)} %row_stats.1), channel_id=2, replica_groups=mesh['x'=4,'z'=8,'core'=2,'head'=4] {'z'}, dimensions={0}, use_global_device_ids=true | all-gather | bytes 313344 | tf_op jit(solution)/shard_map/all_gather | solution.py:233
  130.6 13.0 %row_grads.1 = (bf16[8,144,384]{2,1,0:T(8,128)(2,1)}, bf16[8,272,384]{2,1,0:T(8,128)(2,1)}) custom-call(bf16[32,2,32,384]{3,2,1,0:T(8,128)(2,1)} %bitcast.66, bf16[32,2,32,384]{3,2,1,0:T(8,128)(2,1)} %bitcast.68, bf16[64,384]{1,0:T(8,128)(2,1)} %copy-done.4, bf16[64,384]{1,0:T(8,128)(2,1)} %copy-done.3, bf16[64,384]{1,0:T(8,128)(2,1)} %bitcast.63, ...), custom_call_target="tpu_custom_call" | custom-call | flops 4545576960 | bytes 8388608 | tf_op jit(solution)/shard_map/row_grads/pallas_call | solution.py:130
  143.6 31.7 %all_to_all.21 = bf16[8,272,384]{2,1,0:T(8,128)(2,1)S(1)} all-to-all(bf16[8,272,384]{2,1,0:T(8,128)(2,1)} %get-tuple-element.12), channel_id=1, replica_groups=mesh['x'=4,'z'=8,'core'=2,'head'=4] {'x','core'}, dimensions={0} | all-to-all | bytes 3342336 | tf_op jit(solution)/shard_map/all_to_all | solution.py:236
  175.4 5.4 %all-to-all-start.1 = ((bf16[8,144,384]{2,1,0:T(8,128)(2,1)}), bf16[8,144,384]{2,1,0:T(8,128)(2,1)S(1)}, u32[]{:S(2)}, u32[]{:S(2)}) async-start(bf16[8,144,384]{2,1,0:T(8,128)(2,1)} %get-tuple-element.11), calls=%async_computation.1 | async-start | bytes 1769472 | tf_op jit(solution)/shard_map/all_to_all | solution.py:237
  180.7 0.0 all-reduce.3.cloned.1.call-start
  180.8 0.3 reduce_sum.61
  181.1 0.0 copy-start.7
  181.1 0.0 copy-start.9
  181.1 25.3 %all-to-all-done.1 = bf16[8,144,384]{2,1,0:T(8,128)(2,1)S(1)} async-done(((bf16[8,144,384]{2,1,0:T(8,128)(2,1)}), bf16[8,144,384]{2,1,0:T(8,128)(2,1)S(1)}, u32[]{:S(2)}, u32[]{:S(2)}) %all-to-all-start.1) | async-done | bytes 884768 | tf_op jit(solution)/shard_map/all_to_all | solution.py:237
  206.4 0.1 reduce_sum.60
  206.6 0.0 copy-start.11
  206.6 10.0 %all_to_all.22 = bf16[4,3,32,384]{3,2,1,0:T(8,128)(2,1)S(1)} all-to-all(bf16[4,3,32,384]{3,2,1,0:T(8,128)(2,1)S(1)} %pad_maximum_fusion.1), channel_id=1, replica_groups=mesh['x'=4,'z'=8,'core'=2,'head'=4] {'head'}, dimensions={0} | all-to-all | bytes 589824 | tf_op jit(solution)/shard_map/all_to_all | solution.py:251
  216.6 0.1 copy.52
  216.8 0.0 copy-done
  216.8 0.0 copy-done.9
  216.8 0.0 copy-start.8
  216.8 0.0 copy-start.12
  216.8 1.3 fusion
  218.1 1.4 convolution_bitcast_fusion
  219.5 0.0 all-reduce.3.cloned.1.call-update
  219.6 0.6 fusion.4
  220.2 0.1 multiply_reduce_fusion
  220.3 0.1 bitcast_reduce_fusion
  220.4 0.6 slice.55
  221.0 73.3 %psum.23 = f32[12]{0:T(128)S(1)} all-reduce(f32[12]{0:T(128)S(1)} %bitcast_reduce_fusion), channel_id=1, replica_groups=mesh['x'=4,'z'=8,'core'=2,'head'=4] {'x','z','core','head'}, use_global_device_ids=true, to_apply=%region_8.9 | all-reduce | flops 12 | bytes 96 | tf_op jit(solution)/shard_map/psum | solution.py:271
  294.3 0.1 copy.51
  294.4 0.7 copy.58
  295.0 0.1 copy.50
  295.1 0.7 copy.57
  295.7 0.7 select_multiply_fusion
  296.4 173.6 %all-reduce.3.cloned.1.call-done = (f32[3072,64]{0,1:T(8,128)}, f32[64,1536]{1,0:T(8,128)}) async-done(((f32[3072,64]{0,1:T(8,128)}, f32[64,1536]{1,0:T(8,128)}), (f32[3072,64]{0,1:T(8,128)}, f32[64,1536]{1,0:T(8,128)})) %all-reduce.3.cloned.1.call-update) | async-done | bytes 1179664 | tf_op jit(solution)/shard_map/psum | solution.py:271
  470.0 2.1 broadcast_multiply_fusion
  472.1 0.0 copy-done.10
  472.1 0.8 broadcast_multiply_fusion.1
  (16 shorter events, 0.3 us)
Async XLA Ops:
  7.2 209.6 %copy-start = (bf16[3072,64]{0,1:T(8,128)(2,1)S(1)}, bf16[3072,64]{0,1:T(8,128)(2,1)}, u32[]{:S(2)}) copy-start(bf16[3072,64]{0,1:T(8,128)(2,1)} %param.16) | copy-start | bytes 1179652
  7.2 59.0 %all-gather.4.cloned.1.call-start = ((), (), s32[]{:S(2)}) async-start(), calls=%async_computation.4 | async-start | bytes 1769472 | tf_op jit(solution)/shard_map/all_gather | solution.py:204
  27.7 70.6 %all-gather.6.cloned.1.call-start = ((), (), s32[]{:S(2)}) async-start(), calls=%async_computation.5 | async-start | bytes 1769472 | tf_op jit(solution)/shard_map/all_gather | solution.py:204
  29.3 78.7 %copy-start.1 = (bf16[4,1,2,8,384]{4,3,2,1,0:T(8,128)(2,1)}, bf16[4,1,2,8,384]{4,3,2,1,0:T(8,128)(2,1)S(1)}, u32[]{:S(2)}) copy-start(bf16[4,1,2,8,384]{4,3,2,1,0:T(8,128)(2,1)S(1)} %get-tuple-element.26) | copy-start | bytes 147460
  29.3 78.7 %copy-start.2 = (bf16[4,1,2,8,384]{4,3,2,1,0:T(8,128)(2,1)}, bf16[4,1,2,8,384]{4,3,2,1,0:T(8,128)(2,1)S(1)}, u32[]{:S(2)}) copy-start(bf16[4,1,2,8,384]{4,3,2,1,0:T(8,128)(2,1)S(1)} %get-tuple-element.27) | copy-start | bytes 147460
  30.2 77.9 %copy-start.3 = (bf16[64,384]{1,0:T(8,128)(2,1)}, bf16[64,384]{1,0:T(8,128)(2,1)S(1)}, u32[]{:S(2)}) copy-start(bf16[64,384]{1,0:T(8,128)(2,1)S(1)} %get-tuple-element.24.gt) | copy-start | bytes 147460
  30.2 77.9 %copy-start.4 = (bf16[64,384]{1,0:T(8,128)(2,1)}, bf16[64,384]{1,0:T(8,128)(2,1)S(1)}, u32[]{:S(2)}) copy-start(bf16[64,384]{1,0:T(8,128)(2,1)S(1)} %get-tuple-element.25.qt) | copy-start | bytes 147460
  98.3 1.4 copy-start.5
  99.7 1.4 copy-start.6
  175.4 31.0 %all-to-all-start.1 = ((bf16[8,144,384]{2,1,0:T(8,128)(2,1)}), bf16[8,144,384]{2,1,0:T(8,128)(2,1)S(1)}, u32[]{:S(2)}, u32[]{:S(2)}) async-start(bf16[8,144,384]{2,1,0:T(8,128)(2,1)} %get-tuple-element.11), calls=%async_computation.1 | async-start | bytes 1769472 | tf_op jit(solution)/shard_map/all_to_all | solution.py:237
  180.7 289.3 %all-reduce.3.cloned.1.call-start = ((), (), s32[]{:S(2)}) async-start(), calls=%async_computation.6 | async-start | bytes 2359296 | tf_op jit(solution)/shard_map/psum | solution.py:271
  181.1 35.6 %copy-start.7 = (s32[32,1536]{1,0:T(8,128)S(1)}, s32[32,1536]{1,0:T(8,128)}, u32[]{:S(2)}) copy-start(s32[32,1536]{1,0:T(8,128)} %param.20) | copy-start | bytes 589828
  181.1 35.7 %copy-start.9 = (bf16[32,3072]{1,0:T(8,128)(2,1)S(1)}, bf16[32,3072]{1,0:T(8,128)(2,1)}, u32[]{:S(2)}) copy-start(bf16[32,3072]{1,0:T(8,128)(2,1)} %param.15) | copy-start | bytes 589828
  206.6 11.5 %copy-start.11 = (bf16[64,1536]{1,0:T(8,128)(2,1)S(1)}, bf16[64,1536]{1,0:T(8,128)(2,1)}, u32[]{:S(2)}) copy-start(bf16[64,1536]{1,0:T(8,128)(2,1)} %param.17) | copy-start | bytes 589828
  216.8 2.8 copy-start.8
  216.8 3.4 copy-start.12
  470.0 2.1 copy-start.10
Sparse Core Ops, SparseCore 0:
  27.8 38.2 all-gather.3
  68.6 29.6 all-gather.5
  219.7 250.2 all-reduce.2
